TPU v7x, 32 devices: a whole 2x2x4 slice. The times are simulated.
32 devices in a mesh: seq: 8 (over z, y), dp: 4 (over x, core).
Axes of the slice: x: 2, y: 2, z: 4, core: 2. Of those that a mesh axis runs over, the one named last changes fastest.
Arguments:
- query_input: bfloat16 [4, 4096, 2048], P('dp', 'seq'), may hold values from -6 to 6
- key_input: bfloat16 [4, 4096, 2048], P('dp', 'seq'), may hold values from -6 to 6
- value_input: bfloat16 [4, 4096, 2048], P('dp', 'seq'), may hold values from -6 to 6
- grad_output: bfloat16 [4, 4096, 2048], P('dp', 'seq'), may hold values from -6 to 6
- out_weight: bfloat16 [2048, 2048], P(('seq', 'dp')), may hold values from -0.125 to 0.125
- norm_gain: float32 [2048], replicated, may hold values from 0.1 to 1.9
Outputs:
- result: bfloat16 [4, 4096, 2048], P('dp', 'seq')
- grad_query: bfloat16 [4, 4096, 2048], P('dp', 'seq')
- grad_key: bfloat16 [4, 4096, 2048], P('dp', 'seq')
- grad_value: bfloat16 [4, 4096, 2048], P('dp', 'seq')
- grad_weight: float32 [2048, 2048], P(('seq', 'dp'))
All inputs are finite; a program needn't handle non-finite values.
Results may differ from a plain program's by a relative error of at most 0.015.
Values may be sent and summed in bfloat16 or wider, within the bound.
A program may use at most 192 MiB of HBM per device.

v0:
```python
import jax
import jax.numpy as jnp
from jax import lax
from jax.sharding import PartitionSpec as P

HEADS = 16
HEAD_DIM = 128
BLOCK = 512


epsilon = 1e-06


def carried_in(value, axis, join, neutral, backward):
    count, mine = (lax.axis_size(axis), lax.axis_index(axis))
    pieces = lax.all_gather(value, axis)
    if backward:
        pieces = pieces[::-1]
        mine = count - 1 - mine
    total = jnp.full_like(value, 0) + jnp.asarray(neutral, value.dtype)

    def lap(position, total):
        longer = join(total, pieces[position])
        return jnp.where(position < mine, longer, total)

    return lax.fori_loop(0, count - 1, lap, total)


def silu_slope(inputs):
    sigmoid_value = jax.nn.sigmoid(inputs)
    return sigmoid_value * (1.0 + inputs * (1.0 - sigmoid_value))


def add_states(earlier, following):
    return earlier + following


def causal_product(left, right):
    scores = jnp.einsum("ihd,jhd->hij", left, right, preferred_element_type=jnp.float32)
    length_now = left.shape[0]
    causal = jnp.arange(length_now)[:, None] >= jnp.arange(length_now)[None, :]
    return jnp.where(causal[None], scores, 0.0)


def product(form, left, right):
    return jnp.einsum(form, left, right, preferred_element_type=jnp.float32)


def forward_parts(query_block, key_block, value_block, state_low):
    score_block = causal_product(query_block, key_block).astype(jnp.bfloat16)
    inside = product("hij,jhe->ihe", score_block, value_block)
    carried = product("ihd,hde->ihe", query_block, state_low)
    return (inside + carried, score_block)


def forward_only(items):
    return forward_parts(*items)[0]


def backward_core(
    query_block, key_block, value_block, grad_block, state_low, later_low, score_block
):
    grad_scores = causal_product(grad_block, value_block).astype(jnp.bfloat16)
    grad_fq = product("hij,jhd->ihd", grad_scores, key_block) + product(
        "ihe,hde->ihd", grad_block, state_low
    )
    grad_fk = product("hij,ihd->jhd", grad_scores, query_block) + product(
        "jhe,hde->jhd", value_block, later_low
    )
    grad_fv = product("hij,ihe->jhe", score_block, grad_block) + product(
        "jhd,hde->jhe", key_block, later_low
    )
    return (grad_fq, grad_fk, grad_fv)


def backward_again(items):
    query_block, key_block = (items[0], items[1])
    score_block = causal_product(query_block, key_block).astype(jnp.bfloat16)
    return backward_core(*items + (score_block,))


def shards(query_input, key_input, value_input, grad_output, out_weight, norm_gain):
    tokens = query_input.shape[1]
    feature_count = query_input.shape[2]
    blocks = tokens // BLOCK
    query_raw = query_input[0].astype(jnp.float32)
    key_raw = key_input[0].astype(jnp.float32)
    feat_query = jax.nn.silu(query_raw).astype(jnp.bfloat16).reshape(blocks, BLOCK, HEADS, HEAD_DIM)
    feat_key = jax.nn.silu(key_raw).astype(jnp.bfloat16).reshape(blocks, BLOCK, HEADS, HEAD_DIM)
    value_blocks = value_input[0].reshape(blocks, BLOCK, HEADS, HEAD_DIM)
    zero_state = jnp.zeros((HEADS, HEAD_DIM, HEAD_DIM), jnp.float32)
    block_kv = product("bjhd,bjhe->bhde", feat_key, value_blocks)
    local_incl = jnp.cumsum(block_kv, axis=0)
    incoming = carried_in(local_incl[-1], "seq", add_states, zero_state, False)
    prefix = (incoming[None] + (local_incl - block_kv)).astype(jnp.bfloat16)
    full_weight = lax.all_gather(out_weight, ("seq", "dp"), axis=0, tiled=True)
    attention = lax.map(forward_only, (feat_query, feat_key, value_blocks, prefix))
    attention = attention.reshape(tokens, feature_count)
    radius = jnp.sqrt(jnp.mean(attention * attention, axis=-1, keepdims=True) + epsilon)
    normed = attention / radius
    mixed = (normed * norm_gain).astype(jnp.bfloat16)
    result = jnp.dot(mixed, full_weight, preferred_element_type=jnp.float32).astype(jnp.bfloat16)
    grad_result = grad_output[0]
    grad_mixed = lax.dot_general(
        grad_result, full_weight, (((1,), (1,)), ((), ())), preferred_element_type=jnp.float32
    )
    grad_hat = grad_mixed * norm_gain
    grad_att = (grad_hat - normed * jnp.mean(grad_hat * normed, axis=-1, keepdims=True)) / radius
    grad_att = grad_att.astype(jnp.bfloat16).reshape(blocks, BLOCK, HEADS, HEAD_DIM)
    block_grad = product("bihd,bihe->bhde", feat_query, grad_att)
    suffix_incl = jnp.cumsum(block_grad[::-1], axis=0)[::-1]
    incoming_later = carried_in(suffix_incl[0], "seq", add_states, zero_state, True)
    later = (incoming_later[None] + (suffix_incl - block_grad)).astype(jnp.bfloat16)
    grad_fq, grad_fk, grad_fv = lax.map(
        backward_again, (feat_query, feat_key, value_blocks, grad_att, prefix, later)
    )
    grad_query = (grad_fq.reshape(tokens, feature_count) * silu_slope(query_raw)).astype(
        jnp.bfloat16
    )
    grad_key = (grad_fk.reshape(tokens, feature_count) * silu_slope(key_raw)).astype(jnp.bfloat16)
    grad_value = grad_fv.reshape(tokens, feature_count).astype(jnp.bfloat16)
    grad_weight = lax.psum_scatter(
        lax.dot_general(
            mixed, grad_result, (((0,), (0,)), ((), ())), preferred_element_type=jnp.float32
        ),
        ("seq", "dp"),
        scatter_dimension=0,
        tiled=True,
    )
    return (result[None], grad_query[None], grad_key[None], grad_value[None], grad_weight)


def solution(mesh):
    placed = (
        P("dp", "seq", None),
        P("dp", "seq", None),
        P("dp", "seq", None),
        P("dp", "seq", None),
        P(("seq", "dp"), None),
        P(),
    )
    return jax.shard_map(
        shards,
        mesh=mesh,
        in_specs=placed,
        out_specs=(
            P("dp", "seq", None),
            P("dp", "seq", None),
            P("dp", "seq", None),
            P("dp", "seq", None),
            P(("seq", "dp"), None),
        ),
        check_vma=False,
    )
```

profile of v0, /device:TPU:0, one launch (start us, length us, event | category | flops | bytes accessed | tf_op | source)
XLA Modules:
  0.0 562.6 jit_solution(5268455930311172105)
XLA Ops:
  7.2 2.3 copy.64
  13.4 5.4 multiply_convert_fusion.2
  20.1 2.5 fusion.24
  23.6 4.7 select_convert_fusion.1
  28.3 3.2 copy-done.4
  31.5 6.7 %fusion.20 = f32[16,512,128]{1,2,0:T(8,128)} fusion(bf16[16,512,512]{2,1,0:T(8,128)(2,1)S(1)} %select_convert_fusion.1, bf16[512,16,128]{2,1,0:T(8,128)(2,1)} %bitcast.76), kind=kOutput, calls=%fused_computation.43 | convolution fusion | flops 1073741824 | bytes 14680064 | tf_op jit(solution)/shard_map/while/body/eval_jaxpr/hij,jhe->ihe/dot_general | solution.py:46
  38.3 112.1 %all-gather.8.cloned.1.call-done = f32[128,128,128]{2,1,0:T(8,128)} async-done(((f32[16,128,128]{2,1,0:T(8,128)}), f32[128,128,128]{2,1,0:T(8,128)}) %all-gather.8.cloned.1.call-update) | async-done | bytes 8388624 | tf_op jit(solution)/shard_map/all_gather | solution.py:16
  150.3 11.4 %while.18 = (s32[]{:T(128)}, f32[16,128,128]{2,1,0:T(8,128)S(1)}, s32[]{:T(128)}, f32[8,16,128,128]{3,2,1,0:T(8,128)}, s32[]{:T(128)}, /*index=5*/s32[]{:T(128)}) while((s32[]{:T(128)}, f32[16,128,128]{2,1,0:T(8,128)S(1)}, s32[]{:T(128)}, f32[8,16,128,128]{3,2,1,0:T(8,128)}, s32[]{:T(128)}, /*index=5*/s32[]{:T(128)}) %tuple.86), condition=%wide.region_1.2_spmd.clone, body=%wide.region_0.1_spmd.clone.sunk | while | flops 786436 | bytes 3145829 | solution.py:26
  150.3 1.6 add_select_fusion.4
  152.0 1.6 add_select_fusion.4
  153.6 1.6 add_select_fusion.4
  155.2 1.6 add_select_fusion.4
  156.8 1.6 add_select_fusion.4
  158.4 1.6 add_select_fusion.4
  160.1 1.6 add_select_fusion.4
  163.1 5.8 %multiply_reduce_fusion.1 = (f32[512]{0:T(512)S(1)}, f32[512,16,128]{0,2,1:T(8,128)}) fusion(bf16[16,128,128]{2,1,0:T(8,128)(2,1)S(1)} %add_convert_fusion.2, bf16[512,16,128]{2,0,1:T(8,128)(2,1)} %get-tuple-element.274, f32[16,512,128]{1,2,0:T(8,128)} %fusion.20), kind=kOutput, calls=%fused_computation.30 | convolution fusion | flops 271580672 | bytes 11012096 | tf_op jit(solution)/shard_map/while/body/eval_jaxpr/ihd,hde->ihe/dot_general | solution.py:46
  168.9 5.4 copy.41
  174.4 54.5 %all-gather.6.cloned.1.call-done = bf16[2048,2048]{1,0:T(8,128)(2,1)} async-done(((bf16[64,2048]{1,0:T(8,128)(2,1)}), bf16[2048,2048]{1,0:T(8,128)(2,1)}) %all-gather.6.cloned.1.call-update) | async-done | bytes 8388624 | tf_op jit(solution)/shard_map/all_gather | solution.py:96
  228.9 9.3 %multiply_reduce_fusion = (f32[512]{0:T(512)S(1)}, f32[512,2048]{1,0:T(8,128)S(1)}) fusion(f32[2048]{0:T(1024)S(1)} %copy-done.22, f32[512,2048]{1,0:T(8,128)} %copy.41, f32[512]{0:T(512)S(1)} %add_sqrt_fusion, bf16[2048,2048]{1,0:T(8,128)(2,1)} %all-gather.6.cloned.1.call-done, bf16[1,512,2048]{2,1,0:T(8,128)(2,1)S(1)} %copy-done), kind=kOutput, calls=%fused_computation.28 | convolution fusion | flops 4299161088 | bytes 18886656 | tf_op jit(solution)/shard_map/dot_general | solution.py:104
  238.2 2.2 divide_convert_fusion
  240.4 3.9 copy.61
  244.3 3.9 fusion.28
  248.6 2.6 multiply_convert_fusion
  251.2 8.7 %fusion.15 = f32[2048,2048]{1,0:T(8,128)} fusion(bf16[512,2048]{0,1:T(8,128)(2,1)S(1)} %bitcast.86, bf16[1,512,2048]{2,1,0:T(8,128)(2,1)S(1)} %copy-done), kind=kOutput, calls=%fused_computation.37 | convolution fusion | flops 4294967296 | bytes 20971520 | tf_op jit(solution)/shard_map/dot_general | solution.py:123
  261.5 4.6 select_convert_fusion
  266.1 4.9 fusion.26
  271.1 5.0 convolution_add_fusion.1
  276.0 5.7 %copy.46 = f32[1,512,2048]{2,1,0:T(8,128)} copy(f32[1,512,2048]{1,2,0:T(8,128)} %bitcast.82) | data formatting | bytes 8388608 | tf_op jit(solution)/shard_map/reshape | solution.py:117
  281.8 7.6 %fusion.29 = f32[16,128,512]{2,1,0:T(8,128)} fusion(bf16[512,16,128]{0,2,1:T(8,128)(2,1)} %bitcast.71, bf16[16,512,512]{2,1,0:T(8,128)(2,1)} %copy-done.4), kind=kOutput, calls=%fused_computation.57 | convolution fusion | flops 1073741824 | bytes 14680064 | tf_op jit(solution)/shard_map/while/body/eval_jaxpr/hij,ihe->jhe/dot_general | solution.py:46
  290.1 3.5 fusion.27
  294.8 3.0 fusion.6
  297.9 5.8 %fusion.14 = bf16[1,512,2048]{2,1,0:T(8,128)(2,1)} fusion(bf16[2048,2048]{1,0:T(8,128)(2,1)S(1)} %bitcast.90, f32[2048]{0:T(1024)S(1)} %copy-done.22, f32[512,2048]{1,0:T(8,128)S(1)} %copy-done.13, f32[512]{0:T(512)S(1)} %add_sqrt_fusion), kind=kOutput, calls=%fused_computation.34 | convolution fusion | flops 4299161600 | bytes 14690304 | tf_op jit(solution)/shard_map/dot_general | solution.py:102
  303.7 68.3 %all-gather.10.cloned.1.call-done = f32[128,128,128]{2,1,0:T(8,128)} async-done(((f32[16,128,128]{2,1,0:T(8,128)}), f32[128,128,128]{2,1,0:T(8,128)}) %all-gather.10.cloned.1.call-update) | async-done | bytes 8388624 | tf_op jit(solution)/shard_map/all_gather | solution.py:16
  372.0 7.8 %rev.3 = f32[8,16,128,128]{3,2,1,0:T(8,128)} reverse(f32[8,16,128,128]{3,2,1,0:T(8,128)} %bitcast.84), dimensions={0} | reverse | bytes 16777216 | tf_op jit(solution)/shard_map/rev | solution.py:18
  379.7 11.5 %while.19 = (s32[]{:T(128)}, f32[16,128,128]{2,1,0:T(8,128)S(1)}, s32[]{:T(128)}, f32[8,16,128,128]{3,2,1,0:T(8,128)}, s32[]{:T(128)}, /*index=5*/s32[]{:T(128)}) while((s32[]{:T(128)}, f32[16,128,128]{2,1,0:T(8,128)S(1)}, s32[]{:T(128)}, f32[8,16,128,128]{3,2,1,0:T(8,128)}, s32[]{:T(128)}, /*index=5*/s32[]{:T(128)}) %tuple.75), condition=%wide.region_5.6_spmd.clone, body=%wide.region_4.5_spmd.clone.sunk | while | flops 786436 | bytes 3145829 | solution.py:26
  379.7 1.7 add_select_fusion.5
  381.5 1.6 add_select_fusion.5
  383.1 1.6 add_select_fusion.5
  384.7 1.6 add_select_fusion.5
  386.3 1.6 add_select_fusion.5
  388.0 1.6 add_select_fusion.5
  389.6 1.6 add_select_fusion.5
  392.6 4.5 add_convert_fusion
  397.1 4.1 copy.54
  401.2 5.6 convolution_add_fusion
  406.8 5.6 copy.51
  412.3 5.9 %fusion.13 = bf16[1,512,2048]{2,1,0:T(8,128)(2,1)} fusion(f32[1,512,2048]{2,1,0:T(8,128)} %copy.51, bf16[1,512,2048]{2,1,0:T(8,128)(2,1)} %param.11), kind=kLoop, calls=%fused_computation.23 | loop fusion | flops 10485760 | bytes 8388608 | tf_op jit(solution)/shard_map/convert_element_type | solution.py:120
  418.2 137.4 %reduce-scatter.2.cloned.1.call-done = f32[64,2048]{1,0:T(8,128)} async-done(((f32[2048,2048]{1,0:T(8,128)}), f32[64,2048]{1,0:T(8,128)}) %reduce-scatter.2.cloned.1.call-update) | async-done | bytes 524304 | tf_op jit(solution)/shard_map/reduce_scatter | solution.py:122
  (69 shorter events, 12.7 us)
Async XLA Ops:
  7.2 221.7 %copy-start = (bf16[1,512,2048]{2,1,0:T(8,128)(2,1)S(1)}, bf16[1,512,2048]{2,1,0:T(8,128)(2,1)}, u32[]{:S(2)}) copy-start(bf16[1,512,2048]{2,1,0:T(8,128)(2,1)} %param.13) | copy-start | bytes 6291460
  7.2 143.2 %all-gather.8.cloned.1.call-start = ((), (), s32[]{:S(2)}) async-start(), calls=%async_computation.3 | async-start | bytes 9437184 | tf_op jit(solution)/shard_map/all_gather | solution.py:16
  7.2 2.4 copy-start.15
  9.6 9.2 %copy-start.10 = (bf16[64,8,16,128]{3,2,1,0:T(8,128)(2,1)}, bf16[64,8,16,128]{3,2,1,0:T(8,128)(2,1)S(1)}, u32[]{:S(2)}) copy-start(bf16[64,8,16,128]{3,2,1,0:T(8,128)(2,1)S(1)} %copy.64) | copy-start | bytes 6291460
  10.1 1.8 copy-start.17
  18.8 1.3 copy-start.7
  22.6 206.3 %all-gather.6.cloned.1.call-start = ((), (), s32[]{:S(2)}) async-start(), calls=%async_computation.1 | async-start | bytes 8650752 | tf_op jit(solution)/shard_map/all_gather | solution.py:96
  23.3 348.7 %all-gather.10.cloned.1.call-start = ((), (), s32[]{:S(2)}) async-start(), calls=%async_computation.4 | async-start | bytes 9437184 | tf_op jit(solution)/shard_map/all_gather | solution.py:16
  28.3 3.2 copy-start.4
  163.1 5.9 %copy-start.18 = (bf16[16,128,128]{2,1,0:T(8,128)(2,1)}, bf16[16,128,128]{2,1,0:T(8,128)(2,1)S(1)}, u32[]{:S(2)}) copy-start(bf16[16,128,128]{2,1,0:T(8,128)(2,1)S(1)} %add_convert_fusion.2) | copy-start | bytes 1572868
  168.9 59.9 %copy-start.22 = (f32[2048]{0:T(1024)S(1)}, f32[2048]{0:T(1024)}, u32[]{:S(2)}) copy-start(f32[2048]{0:T(1024)} %param.15) | copy-start | bytes 24580
  228.9 9.3 %copy-start.12 = (f32[512,2048]{1,0:T(8,128)S(1)}, f32[512,2048]{1,0:T(8,128)}, u32[]{:S(2)}) copy-start(f32[512,2048]{1,0:T(8,128)} %copy.41) | copy-start | bytes 12582916
  248.3 307.3 %reduce-scatter.2.cloned.1.call-start = ((), (), s32[]{:S(2)}) async-start(), calls=%async_computation.2 | async-start | bytes 17301504 | tf_op jit(solution)/shard_map/reduce_scatter | solution.py:122
  259.9 1.6 copy-start.6
  261.5 4.6 copy-start.8
  266.1 4.9 copy-start.2
  266.1 4.9 copy-start.19
  281.7 7.6 %copy-start.3 = (bf16[16,512,512]{2,1,0:T(8,128)(2,1)S(1)}, bf16[16,512,512]{2,1,0:T(8,128)(2,1)}, u32[]{:S(2)}) copy-start(bf16[16,512,512]{2,1,0:T(8,128)(2,1)} %copy-done.2) | copy-start | bytes 25165828
  281.7 8.3 %copy-start.5 = (bf16[512,16,128]{2,0,1:T(8,128)(2,1)S(1)}, bf16[512,16,128]{2,0,1:T(8,128)(2,1)}, u32[]{:S(2)}) copy-start(bf16[512,16,128]{2,0,1:T(8,128)(2,1)} %get-tuple-element.274) | copy-start | bytes 6291460
  281.7 16.1 %slice-start = ((s8[8388608]{0:T(1024)(128)(4,1)}), s8[4194304]{0:T(1024)(128)(4,1)S(1)}, s32[]{:S(2)}) async-start(s8[8388608]{0:T(1024)(128)(4,1)} %bitcast.89), calls=%async_computation.5 | async-start | bytes 8388608
  290.1 3.6 copy-start.14
  290.1 4.7 copy-start.16
  290.1 7.8 %slice-start.1 = ((s8[8388608]{0:T(1024)(128)(4,1)}), s8[4194304]{0:T(1024)(128)(4,1)S(1)}, s32[]{:S(2)}) async-start(s8[8388608]{0:T(1024)(128)(4,1)} %bitcast.89), calls=%async_computation.6 | async-start | bytes 8388608
  294.8 3.0 copy-start.13
  379.7 12.9 %copy-start.9 = (bf16[512,16,128]{2,0,1:T(8,128)(2,1)S(1)}, bf16[512,16,128]{2,0,1:T(8,128)(2,1)}, u32[]{:S(2)}) copy-start(bf16[512,16,128]{2,0,1:T(8,128)(2,1)} %copy-done.7) | copy-start | bytes 6291460
  392.6 4.5 copy-start.20
  397.1 4.1 copy-start.11
  397.1 4.1 copy-start.21
  406.8 148.9 %copy-start.1 = (bf16[1,512,2048]{2,1,0:T(8,128)(2,1)S(1)}, bf16[1,512,2048]{2,1,0:T(8,128)(2,1)}, u32[]{:S(2)}) copy-start(bf16[1,512,2048]{2,1,0:T(8,128)(2,1)} %param.13) | copy-start | bytes 6291460
Sparse Core Ops, SparseCore 0:
  22.7 127.6 all-gather.7
  153.2 75.6 all-gather.5
  248.4 123.5 all-gather.9
  374.7 180.8 reduce-scatter.1
where the time goes:
time: 570 us; the launch traced here: 563 us
  waiting for transfers between devices  373 us (65%)
  matrix products  83.1 us (15%)
  local copies, waits for them, and re-layouts  45.6 us (8%)
  other arithmetic  45.6 us (8%)
  between operations  14.5 us (3%)
    all_gather x2, waiting for transfers between devices, carried_in(): pieces = lax.all_gather(value, axis)  180 us
    reduce_scatter x1, waiting for transfers between devices, shards(): lax.psum_scatter(lax.dot_general(mixed, grad_result, (((0,), (0,)), ((),...  137 us
    all_gather x1, waiting for transfers between devices, shards(): full_weight = lax.all_gather(out_weight, ('seq', 'dp'), axis=0, tiled=True)  54.5 us
    dot_general x10, matrix products, product(): return jnp.einsum(form, left, right, preferred_element_type=jnp.float32)  50 us
    select_n x14, other arithmetic, lap(): return jnp.where(position < mine, longer, total)  22.6 us
    unnamed x54, local copies, waits for them, and re-layouts  17.2 us
  transfers between devices with their start and end apart: 4, of which 4 were waited for; matrix products, arithmetic and copies ran while one was open for 24% of the time, Pallas kernels for 0%

commit v1 on v0

v1 whole, which is shorter than its diff:
```python
import functools

import jax
import jax.numpy as jnp
from jax import lax
from jax.experimental import pallas as pl
from jax.experimental.pallas import tpu as pltpu
from jax.sharding import PartitionSpec as P

HEAD_DIM = 128
epsilon = 1e-06
MESH = pl.DeviceIdType.MESH
BF16 = jnp.bfloat16
F32 = jnp.float32
VMEM_LIMIT = 48 * 1024 * 1024


def dot(left, right, contract):
    return lax.dot_general(
        left, right, ((contract[:1], contract[1:]), ((), ())), preferred_element_type=F32
    )


def params(**more):
    return pltpu.CompilerParams(vmem_limit_bytes=VMEM_LIMIT, **more)


def head_cols(head):
    return slice(head * HEAD_DIM, (head + 1) * HEAD_DIM)


def causal(rows):
    return lax.broadcasted_iota(jnp.int32, (rows, rows), 0) >= lax.broadcasted_iota(
        jnp.int32, (rows, rows), 1
    )


def state_kernel(group, k_ref, v_ref, fk_ref, state_ref):
    raw = k_ref[...].astype(F32)
    fk = (raw * jax.nn.sigmoid(raw)).astype(BF16)
    fk_ref[...] = fk
    for head in range(group):
        cols = head_cols(head)
        state_ref[cols, :] = dot(fk[:, cols], v_ref[:, cols], (0, 0)).astype(BF16)


def local_state(key, value):
    tokens, features = key.shape
    group = 4
    width = group * HEAD_DIM
    spec = pl.BlockSpec((tokens, width), lambda i: (0, i))
    return pl.pallas_call(
        functools.partial(state_kernel, group),
        grid=(features // width,),
        in_specs=[spec, spec],
        out_specs=[spec, pl.BlockSpec((width, HEAD_DIM), lambda i: (i, 0))],
        out_shape=[
            jax.ShapeDtypeStruct((tokens, features), BF16),
            jax.ShapeDtypeStruct((features, HEAD_DIM), BF16),
        ],
        compiler_params=params(),
        name="local_state",
    )(key, value)


def carry_kernel(count, backward, x_ref, out_ref, got, sums, res, s1, r1, s2, r2):
    me = lax.axis_index("seq")
    part = x_ref.shape[0] // count

    def rows_of(index):
        return pl.ds(pl.multiple_of(index * part, part), part)

    barrier = pltpu.get_barrier_semaphore()
    for step in range(1, count):
        pl.semaphore_signal(
            barrier, inc=1, device_id={"seq": lax.rem(me + step, count)}, device_id_type=MESH
        )
    pl.semaphore_wait(barrier, count - 1)

    def send(step, source, target, send_sem, recv_sem):
        return pltpu.make_async_remote_copy(
            src_ref=source,
            dst_ref=target,
            send_sem=send_sem.at[step],
            recv_sem=recv_sem.at[step],
            device_id={"seq": lax.rem(me + step, count)},
            device_id_type=MESH,
        )

    first = []
    for step in range(1, count):
        peer = lax.rem(me + step, count)
        copy = send(step, x_ref.at[rows_of(peer)], got.at[me], s1, r1)
        copy.start()
        first.append(copy)
    got[me] = x_ref[rows_of(me), :]
    for copy in first:
        copy.wait_recv()
    total = jnp.zeros((part, x_ref.shape[1]), F32)
    order = range(count)
    for position in reversed(order) if backward else order:
        sums[position] = total.astype(BF16)
        total = total + got[position].astype(F32)
    second = []
    for step in range(1, count):
        peer = lax.rem(me + step, count)
        copy = send(step, sums.at[peer], res.at[rows_of(me)], s2, r2)
        copy.start()
        second.append(copy)
    res[rows_of(me), :] = sums[me]
    for copy in first:
        copy.wait_send()
    for copy in second:
        copy.wait_recv()
    out_ref[...] = res[...]
    for copy in second:
        copy.wait_send()


def carried(state, backward):
    count = lax.axis_size("seq")
    rows, cols = state.shape
    vmem = pl.BlockSpec(memory_space=pltpu.VMEM)
    sems = [pltpu.SemaphoreType.DMA((count,))] * 4
    return pl.pallas_call(
        functools.partial(carry_kernel, count, backward),
        in_specs=[vmem],
        out_specs=vmem,
        out_shape=jax.ShapeDtypeStruct((rows, cols), BF16),
        scratch_shapes=[
            pltpu.VMEM((count, rows // count, cols), BF16),
            pltpu.VMEM((count, rows // count, cols), BF16),
            pltpu.VMEM((rows, cols), BF16),
        ]
        + sems,
        compiler_params=params(collective_id=int(backward), has_side_effects=True),
        name="carry_later" if backward else "carry_earlier",
    )(state)


def forward_kernel(
    group, q_ref, fk_ref, v_ref, state_ref, gain_ref, fq_ref, mixed_ref, normed_ref, radius_ref,
    att, squares,
):
    step = pl.program_id(0)
    rows = q_ref.shape[0]
    raw = q_ref[...].astype(F32)
    fq = (raw * jax.nn.sigmoid(raw)).astype(BF16)
    fq_ref[...] = fq
    keep = causal(rows)

    @pl.when(step == 0)
    def _():
        squares[...] = jnp.zeros_like(squares)

    width = group * HEAD_DIM
    for head in range(group):
        cols = head_cols(head)
        scores = dot(fq[:, cols], fk_ref[:, cols], (1, 1))
        scores = jnp.where(keep, scores, 0.0).astype(BF16)
        out = dot(scores, v_ref[:, cols], (1, 0)) + dot(fq[:, cols], state_ref[cols, :], (1, 0))
        start = pl.multiple_of(step * width + head * HEAD_DIM, HEAD_DIM)
        att[:, pl.ds(start, HEAD_DIM)] = out
        squares[...] += out * out

    @pl.when(step == pl.num_programs(0) - 1)
    def _():
        features = att.shape[1]
        mean = jnp.sum(squares[...], axis=-1, keepdims=True) / features
        radius = jnp.sqrt(mean + epsilon)
        radius_ref[...] = jnp.broadcast_to(radius, radius_ref.shape)
        inverse = 1.0 / radius
        for start in range(0, features, 256):
            cols = slice(start, start + 256)
            normed = att[:, cols] * inverse
            normed_ref[:, cols] = normed.astype(BF16)
            mixed_ref[:, cols] = (normed * gain_ref[:, cols]).astype(BF16)


def forward(query, fk, value, state, gain):
    tokens, features = query.shape
    group = 2
    width = group * HEAD_DIM
    spec = pl.BlockSpec((tokens, width), lambda i: (0, i))
    whole = pl.BlockSpec((tokens, features), lambda i: (0, 0))
    wide = jax.ShapeDtypeStruct((tokens, features), BF16)
    return pl.pallas_call(
        functools.partial(forward_kernel, group),
        grid=(features // width,),
        in_specs=[
            spec,
            spec,
            spec,
            pl.BlockSpec((width, HEAD_DIM), lambda i: (i, 0)),
            pl.BlockSpec((1, features), lambda i: (0, 0)),
        ],
        out_specs=[spec, whole, whole, pl.BlockSpec((tokens, HEAD_DIM), lambda i: (0, 0))],
        out_shape=[wide, wide, wide, jax.ShapeDtypeStruct((tokens, HEAD_DIM), F32)],
        scratch_shapes=[pltpu.VMEM((tokens, features), F32), pltpu.VMEM((tokens, HEAD_DIM), F32)],
        compiler_params=params(),
        name="forward",
    )(query, fk, value, state, gain)


def project_kernel(
    go_ref, mixed_ref, normed_ref, radius_ref, fq_ref, weight_ref, gain_ref,
    result_ref, ga_ref, state_ref, total,
):
    step = pl.program_id(0)
    features = mixed_ref.shape[1]
    grad_mixed = dot(go_ref[...], weight_ref[...], (1, 1))
    grad_hat = grad_mixed * gain_ref[...]
    normed = normed_ref[...].astype(F32)
    inner = jnp.mean(grad_hat * normed, axis=-1, keepdims=True)
    inverse = 1.0 / radius_ref[:, :1]
    grad_att = ((grad_hat - normed * inner) * inverse).astype(BF16)
    ga_ref[...] = grad_att

    @pl.when(step == 0)
    def _():
        total[...] = jnp.zeros_like(total)

    for head in range(features // HEAD_DIM):
        cols = head_cols(head)
        total[cols, :] += dot(fq_ref[:, cols], grad_att[:, cols], (0, 0))
    result_ref[...] = dot(mixed_ref[...], weight_ref[...], (1, 0)).astype(BF16)

    @pl.when(step == pl.num_programs(0) - 1)
    def _():
        state_ref[...] = total[...].astype(BF16)


def project(grad_output, mixed, normed, radius, fq, weight, gain):
    tokens, features = mixed.shape
    out_cols = weight.shape[1]
    rows = 256
    narrow = pl.BlockSpec((rows, features), lambda i: (i, 0))
    outs = pl.BlockSpec((rows, out_cols), lambda i: (i, 0))
    whole = lambda i: (0, 0)
    return pl.pallas_call(
        project_kernel,
        grid=(tokens // rows,),
        in_specs=[
            outs,
            narrow,
            narrow,
            pl.BlockSpec((rows, HEAD_DIM), lambda i: (i, 0)),
            narrow,
            pl.BlockSpec(weight.shape, whole),
            pl.BlockSpec((1, features), whole),
        ],
        out_specs=[outs, narrow, pl.BlockSpec((features, HEAD_DIM), whole)],
        out_shape=[
            jax.ShapeDtypeStruct((tokens, out_cols), BF16),
            jax.ShapeDtypeStruct((tokens, features), BF16),
            jax.ShapeDtypeStruct((features, HEAD_DIM), BF16),
        ],
        scratch_shapes=[pltpu.VMEM((features, HEAD_DIM), F32)],
        compiler_params=params(),
        name="project",
    )(grad_output, mixed, normed, radius, fq, weight, gain)


def backward_kernel(
    group, q_ref, k_ref, v_ref, ga_ref, state_ref, later_ref, gq_ref, gk_ref, gv_ref
):
    rows = q_ref.shape[0]
    keep = causal(rows)
    for head in range(group):
        cols = head_cols(head)
        q_raw = q_ref[:, cols].astype(F32)
        k_raw = k_ref[:, cols].astype(F32)
        q_sig = jax.nn.sigmoid(q_raw)
        k_sig = jax.nn.sigmoid(k_raw)
        fq = (q_raw * q_sig).astype(BF16)
        fk = (k_raw * k_sig).astype(BF16)
        value = v_ref[:, cols]
        grad = ga_ref[:, cols]
        state = state_ref[cols, :]
        later = later_ref[cols, :]
        scores = jnp.where(keep, dot(fq, fk, (1, 1)), 0.0).astype(BF16)
        grad_scores = jnp.where(keep, dot(grad, value, (1, 1)), 0.0).astype(BF16)
        grad_fq = dot(grad_scores, fk, (1, 0)) + dot(grad, state, (1, 1))
        grad_fk = dot(grad_scores, fq, (0, 0)) + dot(value, later, (1, 1))
        grad_v = dot(scores, grad, (0, 0)) + dot(fk, later, (1, 0))
        gq_ref[:, cols] = (grad_fq * (q_sig * (1.0 + q_raw * (1.0 - q_sig)))).astype(BF16)
        gk_ref[:, cols] = (grad_fk * (k_sig * (1.0 + k_raw * (1.0 - k_sig)))).astype(BF16)
        gv_ref[:, cols] = grad_v.astype(BF16)


def backward(query, key, value, grad_att, state, later):
    tokens, features = query.shape
    group = 2
    width = group * HEAD_DIM
    spec = pl.BlockSpec((tokens, width), lambda i: (0, i))
    square = pl.BlockSpec((width, HEAD_DIM), lambda i: (i, 0))
    return pl.pallas_call(
        functools.partial(backward_kernel, group),
        grid=(features // width,),
        in_specs=[spec, spec, spec, spec, square, square],
        out_specs=[spec, spec, spec],
        out_shape=[jax.ShapeDtypeStruct((tokens, features), BF16)] * 3,
        compiler_params=params(),
        name="backward",
    )(query, key, value, grad_att, state, later)


def shards(query_input, key_input, value_input, grad_output, out_weight, norm_gain):
    query, key, value, grad_result = (
        query_input[0], key_input[0], value_input[0], grad_output[0]
    )
    gain = norm_gain[None]
    full_weight = lax.all_gather(out_weight, ("seq", "dp"), axis=0, tiled=True)
    fk, state = local_state(key, value)
    earlier = carried(state, False)
    fq, mixed, normed, radius = forward(query, fk, value, earlier, gain)
    term = lax.dot_general(
        mixed, grad_result, (((0,), (0,)), ((), ())), preferred_element_type=F32
    ).astype(BF16)
    grad_weight = lax.psum_scatter(term, ("seq", "dp"), scatter_dimension=0, tiled=True)
    result, grad_att, grad_state = project(
        grad_result, mixed, normed, radius, fq, full_weight, gain
    )
    later = carried(grad_state, True)
    grad_query, grad_key, grad_value = backward(query, key, value, grad_att, earlier, later)
    return (
        result[None], grad_query[None], grad_key[None], grad_value[None],
        grad_weight.astype(F32),
    )


def solution(mesh):
    rows = P("dp", "seq", None)
    weight = P(("seq", "dp"), None)
    return jax.shard_map(
        shards,
        mesh=mesh,
        in_specs=(rows, rows, rows, rows, weight, P()),
        out_specs=(rows, rows, rows, rows, weight),
        check_vma=False,
    )
```

time: 570 us -> 262 us (0.46); the launches traced: 563 us -> 261 us
  waiting for transfers between devices: 373 us -> 119 us
  Pallas kernels: 0 us -> 112 us
  matrix products: 83.1 us -> 7.3 us
  other arithmetic: 45.6 us -> 1.78 us
  local copies, waits for them, and re-layouts: 45.6 us -> 6.92 us
    all_gather x2 -> x0, waiting for transfers between devices: 180 us -> none  [carried_in(): pieces = lax.all_gather(value, axis)]
    pallas_call x0 -> x6, Pallas kernels: none -> 112 us  [the longest x2 62.9 us: carried(): pl.pallas_call(functools.partial(carry_kernel, count, backward), in_specs...]
    dot_general x14 -> x0, matrix products: 74.4 us -> none  [the longest x10 50 us: product(): return jnp.einsum(form, left, right, preferred_element_type=jnp.float32)]
    reduce_scatter x1, waiting for transfers between devices: 137 us -> 90.5 us  [shards(): lax.psum_scatter(term, ('seq', 'dp'), scatter_dimension=0, tiled=True)]
    all_gather x1, waiting for transfers between devices: 54.5 us -> 28.1 us  [shards(): full_weight = lax.all_gather(out_weight, ('seq', 'dp'), axis=0, tiled=True)]
    select_n x14 -> x0, other arithmetic: 22.6 us -> none  [lap(): return jnp.where(position < mine, longer, total)]
    convert_element_type x7 -> x1, other arithmetic: 21.9 us -> 1.78 us  [shards(): grad_weight.astype(F32)]
    reshape x3 -> x0, local copies, waits for them, and re-layouts: 16.7 us -> none  [the longest x1 5.68 us: shards(): grad_fq.reshape(tokens, feature_count) * silu_slope(query_raw)]
  transfers between devices with their start and end apart: 4 -> 2, of which waited for: 4 -> 2; matrix products, arithmetic and copies ran while one was open for 24% -> 3% of each run, Pallas kernels for 0% -> 43%
where the time goes in v1:
time: 262 us; the launch traced here: 261 us
  waiting for transfers between devices  119 us (45%)
  Pallas kernels  112 us (43%)
  between operations  14.1 us (5%)
  matrix products  7.3 us (3%)
  local copies, waits for them, and re-layouts  6.92 us (3%)
    reduce_scatter x1, waiting for transfers between devices, shards(): lax.psum_scatter(term, ('seq', 'dp'), scatter_dimension=0, tiled=True)  90.5 us
    pallas_call x2, Pallas kernels, carried(): pl.pallas_call(functools.partial(carry_kernel, count, backward), in_specs...  62.9 us
    all_gather x1, waiting for transfers between devices, shards(): full_weight = lax.all_gather(out_weight, ('seq', 'dp'), axis=0, tiled=True)  28.1 us
    pallas_call x1, Pallas kernels, project(): pl.pallas_call(project_kernel, grid=(tokens // rows,), in_specs=[outs, na...  17.2 us
    pallas_call x1, Pallas kernels, backward(): pl.pallas_call(functools.partial(backward_kernel, group), grid=(features...  16.7 us
    pallas_call x1, Pallas kernels, forward(): pl.pallas_call(functools.partial(forward_kernel, group), grid=(features /...  11.5 us
    dot_general x1, matrix products, shards(): lax.dot_general(mixed, grad_result, (((0,), (0,)), ((), ())), preferred_e...  7.3 us
    unnamed x18, local copies, waits for them, and re-layouts  6.92 us
  transfers between devices with their start and end apart: 2, of which 2 were waited for; matrix products, arithmetic and copies ran while one was open for 3% of the time, Pallas kernels for 43%

profile of v1, /device:TPU:0, one launch (start us, length us, event | category | flops | bytes accessed | tf_op | source)
XLA Modules:
  0.0 261.4 jit_solution(1005495943757906357)
XLA Ops:
  7.2 0.0 all-gather.2.cloned.1.call-start
  7.2 0.7 all-gather.2.cloned.1.call-update
  7.9 0.0 reduce-scatter.2.cloned.1.call-start
  7.9 0.0 copy-start
  8.0 1.6 copy-done
  9.5 0.0 copy-start.8
  9.5 3.6 %local_state.1 = (bf16[512,2048]{1,0:T(8,128)(2,1)S(1)}, bf16[2048,128]{1,0:T(8,128)(2,1)S(1)}) custom-call(bf16[512,2048]{1,0:T(8,128)(2,1)S(1)} %bitcast.12, bf16[512,2048]{1,0:T(8,128)(2,1)} %bitcast.19), custom_call_target="tpu_custom_call" | custom-call | tf_op jit(solution)/shard_map/local_state/pallas_call | solution.py:52
  13.2 0.0 copy-start.4
  13.2 1.3 copy-done.4
  14.5 34.4 %carry_earlier.1.state_ref = bf16[2048,128]{1,0:T(8,128)(2,1)S(1)} custom-call(bf16[2048,128]{1,0:T(8,128)(2,1)S(1)} %get-tuple-element.18.x_ref), custom_call_target="tpu_custom_call" | custom-call | tf_op jit(solution)/shard_map/carry_earlier/pallas_call | solution.py:125
  48.9 0.0 copy-done.8
  48.9 0.0 copy-start.5
  48.9 11.5 %forward.1 = (bf16[512,2048]{1,0:T(8,128)(2,1)S(1)}, bf16[512,2048]{1,0:T(8,128)(2,1)S(1)}, bf16[512,2048]{1,0:T(8,128)(2,1)}, f32[512,128]{1,0:T(8,128)S(1)}) custom-call(bf16[512,2048]{1,0:T(8,128)(2,1)} %bitcast.14, bf16[512,2048]{1,0:T(8,128)(2,1)} %copy-done.4, bf16[512,2048]{1,0:T(8,128)(2,1)} %bitcast.20, ...), custom_call_target="tpu_custom_call" | custom-call | tf_op jit(solution)/shard_map/forward/pallas_call | solution.py:187
  60.4 0.0 copy-start.6
  60.4 1.3 copy-done.6
  61.7 0.0 copy-start.7
  61.7 1.3 copy-done.7
  63.1 0.0 copy-done.5
  63.1 7.3 %convolution_convert_fusion = bf16[2048,2048]{1,0:T(8,128)(2,1)} fusion(bf16[512,2048]{1,0:T(8,128)(2,1)S(1)} %get-tuple-element.19.mixed_ref, bf16[1,512,2048]{2,1,0:T(8,128)(2,1)S(1)} %copy-done.5), kind=kOutput, calls=%fused_computation | convolution fusion | flops 4299161600 | bytes 12582912 | tf_op jit(solution)/shard_map/dot_general | solution.py:317
  70.4 0.0 reduce-scatter.2.cloned.1.call-update
  70.4 28.1 %all-gather.2.cloned.1.call-done.weight_ref = bf16[2048,2048]{1,0:T(8,128)(2,1)} async-done(((bf16[64,2048]{1,0:T(8,128)(2,1)}), bf16[2048,2048]{1,0:T(8,128)(2,1)}) %all-gather.2.cloned.1.call-update) | async-done | bytes 8388624 | tf_op jit(solution)/shard_map/all_gather | solution.py:313
  98.5 0.0 copy-start.1
  98.5 0.0 copy-start.2
  98.5 17.2 %project.1 = (bf16[512,2048]{1,0:T(8,128)(2,1)}, bf16[512,2048]{1,0:T(8,128)(2,1)S(1)}, bf16[2048,128]{1,0:T(8,128)(2,1)S(1)}) custom-call(bf16[512,2048]{1,0:T(8,128)(2,1)S(1)} %bitcast.16, bf16[512,2048]{1,0:T(8,128)(2,1)} %copy-done.7, bf16[512,2048]{1,0:T(8,128)(2,1)} %get-tuple-element.20.normed_ref, f32[512,128]{1,0:T(8,128)S(1)} %get-tuple-element.21.radius_ref, ...), custom_call_target="tpu_custom_call" | custom-call | tf_op jit(solution)/shard_map/project/pallas_call | solution.py:240
  115.6 0.0 copy-start.3
  115.6 1.4 copy-done.3
  117.0 28.5 %carry_later.1.later_ref = bf16[2048,128]{1,0:T(8,128)(2,1)S(1)} custom-call(bf16[2048,128]{1,0:T(8,128)(2,1)S(1)} %get-tuple-element.25.x_ref), custom_call_target="tpu_custom_call" | custom-call | tf_op jit(solution)/shard_map/carry_later/pallas_call | solution.py:125
  145.5 0.0 copy-done.1
  145.6 0.0 copy-done.2
  145.6 16.7 %backward.1 = (bf16[512,2048]{1,0:T(8,128)(2,1)}, bf16[512,2048]{1,0:T(8,128)(2,1)}, bf16[512,2048]{1,0:T(8,128)(2,1)}) custom-call(bf16[512,2048]{1,0:T(8,128)(2,1)S(1)} %bitcast.15, bf16[512,2048]{1,0:T(8,128)(2,1)S(1)} %bitcast.13, bf16[512,2048]{1,0:T(8,128)(2,1)} %bitcast.21, bf16[512,2048]{1,0:T(8,128)(2,1)} %copy-done.3, ...), custom_call_target="tpu_custom_call" | custom-call | tf_op jit(solution)/shard_map/backward/pallas_call | solution.py:297
  162.2 90.5 %reduce-scatter.2.cloned.1.call-done = bf16[64,2048]{1,0:T(8,128)(2,1)} async-done(((bf16[2048,2048]{1,0:T(8,128)(2,1)}), bf16[64,2048]{1,0:T(8,128)(2,1)}) %reduce-scatter.2.cloned.1.call-update) | async-done | bytes 262160 | tf_op jit(solution)/shard_map/reduce_scatter | solution.py:320
  252.8 1.8 convert_element_type.7
Async XLA Ops:
  7.2 91.3 %all-gather.2.cloned.1.call-start = ((), (), s32[]{:S(2)}) async-start(), calls=%async_computation.1 | async-start | bytes 8650752 | tf_op jit(solution)/shard_map/all_gather | solution.py:313
  7.9 244.9 %reduce-scatter.2.cloned.1.call-start = ((), (), s32[]{:S(2)}) async-start(), calls=%async_computation.2 | async-start | bytes 8650752 | tf_op jit(solution)/shard_map/reduce_scatter | solution.py:320
  7.9 1.6 copy-start
  9.5 39.4 %copy-start.8 = (f32[2048]{0:T(1024)S(1)}, f32[2048]{0:T(1024)}, u32[]{:S(2)}) copy-start(f32[2048]{0:T(1024)} %param.11) | copy-start | bytes 24580
  13.2 1.3 copy-start.4
  48.9 14.1 %copy-start.5 = (bf16[1,512,2048]{2,1,0:T(8,128)(2,1)S(1)}, bf16[1,512,2048]{2,1,0:T(8,128)(2,1)}, u32[]{:S(2)}) copy-start(bf16[1,512,2048]{2,1,0:T(8,128)(2,1)} %param.9) | copy-start | bytes 6291460
  60.4 1.3 copy-start.6
  61.7 1.3 copy-start.7
  98.5 47.1 %copy-start.1 = (bf16[1,512,2048]{2,1,0:T(8,128)(2,1)S(1)}, bf16[1,512,2048]{2,1,0:T(8,128)(2,1)}, u32[]{:S(2)}) copy-start(bf16[1,512,2048]{2,1,0:T(8,128)(2,1)} %param.7) | copy-start | bytes 6291460
  98.5 47.1 %copy-start.2 = (bf16[1,512,2048]{2,1,0:T(8,128)(2,1)S(1)}, bf16[1,512,2048]{2,1,0:T(8,128)(2,1)}, u32[]{:S(2)}) copy-start(bf16[1,512,2048]{2,1,0:T(8,128)(2,1)} %param.6) | copy-start | bytes 6291460
  115.6 1.4 copy-start.3
Sparse Core Ops, SparseCore 0:
  10.9 87.5 all-gather.1
  100.8 151.9 reduce-scatter.1

commit v2 on v1

--- a/solution.py
+++ b/solution.py
@@ -305,19 +305,139 @@
     )(query, key, value, grad_att, state, later)
 
 
+def pair_barrier(peer):
+    barrier = pltpu.get_barrier_semaphore()
+    pl.semaphore_signal(barrier, inc=1, device_id={"pair": peer}, device_id_type=MESH)
+    pl.semaphore_wait(barrier, 1)
+
+
+def pair_gather_kernel(x_ref, out_ref, got, send_sem, recv_sem):
+    mine = lax.axis_index("pair")
+    peer = 1 - mine
+    pair_barrier(peer)
+    copy = pltpu.make_async_remote_copy(
+        src_ref=x_ref,
+        dst_ref=got,
+        send_sem=send_sem,
+        recv_sem=recv_sem,
+        device_id={"pair": peer},
+        device_id_type=MESH,
+    )
+    copy.start()
+
+    def own(group, unused):
+        out_ref[group, mine] = x_ref[group]
+        return unused
+
+    def other(group, unused):
+        out_ref[group, peer] = got[group]
+        return unused
+
+    groups = x_ref.shape[0]
+    lax.fori_loop(0, groups, own, 0)
+    copy.wait_recv()
+    lax.fori_loop(0, groups, other, 0)
+    copy.wait_send()
+
+
+def pair_gather(half, part):
+    rows, cols = half.shape
+    groups = rows // part
+    vmem = pl.BlockSpec(memory_space=pltpu.VMEM)
+    whole = pl.pallas_call(
+        pair_gather_kernel,
+        in_specs=[vmem],
+        out_specs=vmem,
+        out_shape=jax.ShapeDtypeStruct((groups, 2, part, cols), BF16),
+        scratch_shapes=[
+            pltpu.VMEM((groups, part, cols), BF16),
+            pltpu.SemaphoreType.DMA,
+            pltpu.SemaphoreType.DMA,
+        ],
+        compiler_params=params(collective_id=2, has_side_effects=True),
+        name="pair_gather",
+    )(half.reshape(groups, part, cols))
+    return whole.reshape(2 * rows, cols)
+
+
+def pair_term_kernel(part, mixed_ref, go_ref, out_ref, keep, away, got, send_sem, recv_sem):
+    mine = lax.axis_index("pair")
+    peer = 1 - mine
+    chunks, rows, cols = out_ref.shape
+    pair_barrier(peer)
+
+    def copy_of(chunk):
+        return pltpu.make_async_remote_copy(
+            src_ref=away.at[chunk],
+            dst_ref=got.at[chunk],
+            send_sem=send_sem.at[chunk],
+            recv_sem=recv_sem.at[chunk],
+            device_id={"pair": peer},
+            device_id_type=MESH,
+        )
+
+    def multiply(chunk, unused):
+        columns = pl.ds(pl.multiple_of(chunk * 2 * rows, 2 * rows), 2 * rows)
+        term = dot(mixed_ref[:, columns], go_ref[...], (0, 0))
+        term = term.reshape(rows // part, 2, part, cols)
+        low = term[:, 0].reshape(rows, cols)
+        high = term[:, 1].reshape(rows, cols)
+        keep[chunk] = jnp.where(mine == 0, low, high)
+        away[chunk] = jnp.where(mine == 0, high, low).astype(BF16)
+        copy_of(chunk).start()
+        return unused
+
+    def add(chunk, unused):
+        copy_of(chunk).wait_recv()
+        out_ref[chunk] = (keep[chunk] + got[chunk].astype(F32)).astype(BF16)
+        return unused
+
+    def sent(chunk, unused):
+        copy_of(chunk).wait_send()
+        return unused
+
+    lax.fori_loop(0, chunks, multiply, 0)
+    lax.fori_loop(0, chunks, add, 0)
+    lax.fori_loop(0, chunks, sent, 0)
+
+
+def pair_term(mixed, grad_output, part):
+    features = mixed.shape[1]
+    cols = grad_output.shape[1]
+    rows = max(HEAD_DIM, part)
+    chunks = features // (2 * rows)
+    vmem = pl.BlockSpec(memory_space=pltpu.VMEM)
+    term = pl.pallas_call(
+        functools.partial(pair_term_kernel, part),
+        in_specs=[vmem, vmem],
+        out_specs=vmem,
+        out_shape=jax.ShapeDtypeStruct((chunks, rows, cols), BF16),
+        scratch_shapes=[
+            pltpu.VMEM((chunks, rows, cols), F32),
+            pltpu.VMEM((chunks, rows, cols), BF16),
+            pltpu.VMEM((chunks, rows, cols), BF16),
+            pltpu.SemaphoreType.DMA((chunks,)),
+            pltpu.SemaphoreType.DMA((chunks,)),
+        ],
+        compiler_params=params(collective_id=3, has_side_effects=True),
+        name="pair_term",
+    )(mixed, grad_output)
+    return term.reshape(chunks * rows, cols)
+
+
 def shards(query_input, key_input, value_input, grad_output, out_weight, norm_gain):
     query, key, value, grad_result = (
         query_input[0], key_input[0], value_input[0], grad_output[0]
     )
     gain = norm_gain[None]
-    full_weight = lax.all_gather(out_weight, ("seq", "dp"), axis=0, tiled=True)
+    part = out_weight.shape[0]
+    half_weight = lax.all_gather(out_weight, ("seq", "outer"), axis=0, tiled=True)
     fk, state = local_state(key, value)
     earlier = carried(state, False)
     fq, mixed, normed, radius = forward(query, fk, value, earlier, gain)
-    term = lax.dot_general(
-        mixed, grad_result, (((0,), (0,)), ((), ())), preferred_element_type=F32
-    ).astype(BF16)
-    grad_weight = lax.psum_scatter(term, ("seq", "dp"), scatter_dimension=0, tiled=True)
+    term = pair_term(mixed, grad_result, part)
+    grad_weight = lax.psum_scatter(term, ("seq", "outer"), scatter_dimension=0, tiled=True)
+    full_weight = pair_gather(half_weight, part)
     result, grad_att, grad_state = project(
         grad_result, mixed, normed, radius, fq, full_weight, gain
     )
@@ -330,11 +450,15 @@
 
 
 def solution(mesh):
-    rows = P("dp", "seq", None)
-    weight = P(("seq", "dp"), None)
+    seq, dp = mesh.shape["seq"], mesh.shape["dp"]
+    paired = jax.sharding.Mesh(
+        mesh.devices.reshape(seq, dp // 2, 2), ("seq", "outer", "pair")
+    )
+    rows = P(("outer", "pair"), "seq", None)
+    weight = P(("seq", "outer", "pair"), None)
     return jax.shard_map(
         shards,
-        mesh=mesh,
+        mesh=paired,
         in_specs=(rows, rows, rows, rows, weight, P()),
         out_specs=(rows, rows, rows, rows, weight),
         check_vma=False,

time: 262 us -> 208 us (0.79)
  the two profiles are of different devices: /device:TPU:0 before, /device:TPU:10 now
where the time goes in v2:
time: 208 us; the launch traced here: 207 us
  Pallas kernels  156 us (75%)
  waiting for transfers between devices  28.6 us (14%)
  between operations  14.2 us (7%)
  local copies, waits for them, and re-layouts  6.46 us (3%)
    pallas_call x2, Pallas kernels, carried(): pl.pallas_call(functools.partial(carry_kernel, count, backward), in_specs...  86.5 us
    all_gather x1, waiting for transfers between devices, shards(): lax.all_gather(out_weight, ('seq', 'outer'), axis=0, tiled=True)  18.5 us
    pallas_call x1, Pallas kernels, project(): pl.pallas_call(project_kernel, grid=(tokens // rows,), in_specs=[outs, na...  17.3 us
    pallas_call x1, Pallas kernels, backward(): pl.pallas_call(functools.partial(backward_kernel, group), grid=(features...  16.7 us
    pallas_call x1, Pallas kernels, forward(): pl.pallas_call(functools.partial(forward_kernel, group), grid=(features /...  11.5 us
    pallas_call x1, Pallas kernels, pair_gather(): pl.pallas_call(pair_gather_kernel, in_specs=[vmem], out_specs=vmem, out_s...  10.7 us
    pallas_call x1, Pallas kernels, pair_term(): pl.pallas_call(functools.partial(pair_term_kernel, part), in_specs=[vmem,...  10.2 us
    reduce_scatter x1, waiting for transfers between devices, shards(): lax.psum_scatter(term, ('seq', 'outer'), scatter_dimension=0, tiled=True)  9.36 us
  transfers between devices with their start and end apart: 2, of which 2 were waited for; matrix products, arithmetic and copies ran while one was open for 0% of the time, Pallas kernels for 75%

profile of v2, /device:TPU:10, one launch (start us, length us, event | category | flops | bytes accessed | tf_op | source)
XLA Modules:
  0.0 207.5 jit_solution(932290899529319787)
XLA Ops:
  7.2 0.0 all-gather.2.cloned.1.call-start
  7.2 0.7 all-gather.2.cloned.1.call-update
  7.9 0.0 reduce-scatter.2.cloned.1.call-start
  7.9 0.0 copy-start
  8.0 1.6 copy-done
  9.5 0.0 copy-start.9
  9.5 3.6 %local_state.1 = (bf16[512,2048]{1,0:T(8,128)(2,1)S(1)}, bf16[2048,128]{1,0:T(8,128)(2,1)S(1)}) custom-call(bf16[512,2048]{1,0:T(8,128)(2,1)S(1)} %bitcast.12, bf16[512,2048]{1,0:T(8,128)(2,1)} %bitcast.22), custom_call_target="tpu_custom_call" | custom-call | tf_op jit(solution)/shard_map/local_state/pallas_call | solution.py:52
  13.2 0.0 copy-start.7
  13.2 1.3 copy-done.7
  14.5 40.4 %carry_earlier.1.state_ref = bf16[2048,128]{1,0:T(8,128)(2,1)S(1)} custom-call(bf16[2048,128]{1,0:T(8,128)(2,1)S(1)} %get-tuple-element.18.x_ref), custom_call_target="tpu_custom_call" | custom-call | tf_op jit(solution)/shard_map/carry_earlier/pallas_call | solution.py:125
  54.9 0.0 copy-done.9
  54.9 0.0 copy-start.3
  54.9 11.5 %forward.1 = (bf16[512,2048]{1,0:T(8,128)(2,1)S(1)}, bf16[512,2048]{1,0:T(8,128)(2,1)S(1)}, bf16[512,2048]{1,0:T(8,128)(2,1)}, f32[512,128]{1,0:T(8,128)S(1)}) custom-call(bf16[512,2048]{1,0:T(8,128)(2,1)} %bitcast.14, bf16[512,2048]{1,0:T(8,128)(2,1)} %copy-done.7, bf16[512,2048]{1,0:T(8,128)(2,1)} %bitcast.23, ...), custom_call_target="tpu_custom_call" | custom-call | tf_op jit(solution)/shard_map/forward/pallas_call | solution.py:187
  66.4 0.0 copy-start.4
  66.4 0.0 copy-start.8
  66.4 0.0 copy-done.3
  66.4 10.2 %pair_term.1 = bf16[8,128,2048]{2,1,0:T(8,128)(2,1)} custom-call(bf16[512,2048]{1,0:T(8,128)(2,1)S(1)} %get-tuple-element.19.mixed_ref, bf16[512,2048]{1,0:T(8,128)(2,1)S(1)} %bitcast.16), custom_call_target="tpu_custom_call" | custom-call | tf_op jit(solution)/shard_map/pair_term/pallas_call | solution.py:410
  76.6 0.0 copy-done.4
  76.6 0.0 copy-done.8
  76.6 0.0 reduce-scatter.2.cloned.1.call-update
  76.6 18.5 %all-gather.2.cloned.1.call-done = bf16[1024,2048]{1,0:T(8,128)(2,1)} async-done(((bf16[64,2048]{1,0:T(8,128)(2,1)}), bf16[1024,2048]{1,0:T(8,128)(2,1)}) %all-gather.2.cloned.1.call-update) | async-done | bytes 4194320 | tf_op jit(solution)/shard_map/all_gather | solution.py:434
  95.2 0.0 copy-start.5
  95.2 2.2 %copy-done.5 = bf16[1024,2048]{1,0:T(8,128)(2,1)S(1)} copy-done((bf16[1024,2048]{1,0:T(8,128)(2,1)S(1)}, bf16[1024,2048]{1,0:T(8,128)(2,1)}, u32[]{:S(2)}) %copy-start.5) | copy-done | bytes 4194328
  97.4 10.7 %pair_gather.1 = bf16[16,2,64,2048]{3,2,1,0:T(8,128)(2,1)} custom-call(bf16[16,64,2048]{2,1,0:T(8,128)(2,1)S(1)} %bitcast.18), custom_call_target="tpu_custom_call" | custom-call | tf_op jit(solution)/shard_map/pair_gather/pallas_call | solution.py:347
  108.1 0.0 copy-start.1
  108.1 0.0 copy-start.2
  108.1 17.3 %project.1 = (bf16[512,2048]{1,0:T(8,128)(2,1)}, bf16[512,2048]{1,0:T(8,128)(2,1)S(1)}, bf16[2048,128]{1,0:T(8,128)(2,1)S(1)}) custom-call(bf16[512,2048]{1,0:T(8,128)(2,1)S(1)} %bitcast.17, bf16[512,2048]{1,0:T(8,128)(2,1)} %copy-done.4, bf16[512,2048]{1,0:T(8,128)(2,1)} %get-tuple-element.20.normed_ref, f32[512,128]{1,0:T(8,128)S(1)} %get-tuple-element.21.radius_ref, ...), custom_call_target="tpu_custom_call" | custom-call | tf_op jit(solution)/shard_map/project/pallas_call | solution.py:240
  125.4 0.0 copy-start.6
  125.4 1.3 copy-done.6
  126.7 46.1 %carry_later.1.later_ref = bf16[2048,128]{1,0:T(8,128)(2,1)S(1)} custom-call(bf16[2048,128]{1,0:T(8,128)(2,1)S(1)} %get-tuple-element.25.x_ref), custom_call_target="tpu_custom_call" | custom-call | tf_op jit(solution)/shard_map/carry_later/pallas_call | solution.py:125
  172.8 0.0 copy-done.1
  172.8 0.0 copy-done.2
  172.9 16.7 %backward.1 = (bf16[512,2048]{1,0:T(8,128)(2,1)}, bf16[512,2048]{1,0:T(8,128)(2,1)}, bf16[512,2048]{1,0:T(8,128)(2,1)}) custom-call(bf16[512,2048]{1,0:T(8,128)(2,1)S(1)} %bitcast.15, bf16[512,2048]{1,0:T(8,128)(2,1)S(1)} %bitcast.13, bf16[512,2048]{1,0:T(8,128)(2,1)} %bitcast.24, bf16[512,2048]{1,0:T(8,128)(2,1)} %copy-done.6, ...), custom_call_target="tpu_custom_call" | custom-call | tf_op jit(solution)/shard_map/backward/pallas_call | solution.py:297
  189.5 9.4 %reduce-scatter.2.cloned.1.call-done = bf16[64,2048]{1,0:T(8,128)(2,1)} async-done(((bf16[1024,2048]{1,0:T(8,128)(2,1)}), bf16[64,2048]{1,0:T(8,128)(2,1)}) %reduce-scatter.2.cloned.1.call-update) | async-done | bytes 262160 | tf_op jit(solution)/shard_map/reduce_scatter | solution.py:439
  198.9 1.8 convert_element_type.3
Async XLA Ops:
  7.2 88.0 %all-gather.2.cloned.1.call-start = ((), (), s32[]{:S(2)}) async-start(), calls=%async_computation.1 | async-start | bytes 4456448 | tf_op jit(solution)/shard_map/all_gather | solution.py:434
  7.9 191.0 %reduce-scatter.2.cloned.1.call-start = ((), (), s32[]{:S(2)}) async-start(), calls=%async_computation.2 | async-start | bytes 4456448 | tf_op jit(solution)/shard_map/reduce_scatter | solution.py:439
  7.9 1.6 copy-start
  9.5 45.3 %copy-start.9 = (f32[2048]{0:T(1024)S(1)}, f32[2048]{0:T(1024)}, u32[]{:S(2)}) copy-start(f32[2048]{0:T(1024)} %param.11) | copy-start | bytes 24580
  13.2 1.3 copy-start.7
  54.9 11.5 %copy-start.3 = (bf16[1,512,2048]{2,1,0:T(8,128)(2,1)S(1)}, bf16[1,512,2048]{2,1,0:T(8,128)(2,1)}, u32[]{:S(2)}) copy-start(bf16[1,512,2048]{2,1,0:T(8,128)(2,1)} %param.9) | copy-start | bytes 6291460
  66.4 10.2 %copy-start.4 = (bf16[512,2048]{1,0:T(8,128)(2,1)}, bf16[512,2048]{1,0:T(8,128)(2,1)S(1)}, u32[]{:S(2)}) copy-start(bf16[512,2048]{1,0:T(8,128)(2,1)S(1)} %get-tuple-element.19.mixed_ref) | copy-start | bytes 6291460
  66.4 10.3 %copy-start.8 = (bf16[512,2048]{1,0:T(8,128)(2,1)}, bf16[512,2048]{1,0:T(8,128)(2,1)S(1)}, u32[]{:S(2)}) copy-start(bf16[512,2048]{1,0:T(8,128)(2,1)S(1)} %get-tuple-element.22.fq_ref) | copy-start | bytes 6291460
  95.2 2.2 %copy-start.5 = (bf16[1024,2048]{1,0:T(8,128)(2,1)S(1)}, bf16[1024,2048]{1,0:T(8,128)(2,1)}, u32[]{:S(2)}) copy-start(bf16[1024,2048]{1,0:T(8,128)(2,1)} %all-gather.2.cloned.1.call-done) | copy-start | bytes 12582916
  108.1 64.8 %copy-start.1 = (bf16[1,512,2048]{2,1,0:T(8,128)(2,1)S(1)}, bf16[1,512,2048]{2,1,0:T(8,128)(2,1)}, u32[]{:S(2)}) copy-start(bf16[1,512,2048]{2,1,0:T(8,128)(2,1)} %param.7) | copy-start | bytes 6291460
  108.1 64.8 %copy-start.2 = (bf16[1,512,2048]{2,1,0:T(8,128)(2,1)S(1)}, bf16[1,512,2048]{2,1,0:T(8,128)(2,1)}, u32[]{:S(2)}) copy-start(bf16[1,512,2048]{2,1,0:T(8,128)(2,1)} %param.6) | copy-start | bytes 6291460
  125.4 1.3 copy-start.6
Sparse Core Ops, SparseCore 0:
  10.8 84.3 all-gather.1
  97.5 101.3 reduce-scatter.1

commit v3 on v2

--- a/solution.py
+++ b/solution.py
@@ -63,7 +63,21 @@
     )(key, value)
 
 
-def carry_kernel(count, backward, x_ref, out_ref, got, sums, res, s1, r1, s2, r2):
+def carry_kernel(count, backward, *refs):
+    if backward:
+        x_ref, mixed_ref, weight_ref, out_ref, result_ref = refs[:5]
+    else:
+        x_ref, out_ref = refs[:2]
+    got, sums, res, s1, r1, s2, r2 = refs[-7:]
+
+    def results(begin, end):
+        def tile(index, unused):
+            columns = pl.ds(pl.multiple_of(index * 256, 256), 256)
+            result_ref[:, columns] = dot(mixed_ref[...], weight_ref[:, columns], (1, 0)).astype(BF16)
+            return unused
+
+        lax.fori_loop(begin, end, tile, 0)
+
     me = lax.axis_index("seq")
     part = x_ref.shape[0] // count
 
@@ -94,6 +108,9 @@
         copy.start()
         first.append(copy)
     got[me] = x_ref[rows_of(me), :]
+    if backward:
+        tiles = weight_ref.shape[1] // 256
+        results(0, tiles // 2)
     for copy in first:
         copy.wait_recv()
     total = jnp.zeros((part, x_ref.shape[1]), F32)
@@ -108,6 +125,8 @@
         copy.start()
         second.append(copy)
     res[rows_of(me), :] = sums[me]
+    if backward:
+        results(tiles // 2, tiles)
     for copy in first:
         copy.wait_send()
     for copy in second:
@@ -117,16 +136,20 @@
         copy.wait_send()
 
 
-def carried(state, backward):
+def carried(state, backward, *product):
     count = lax.axis_size("seq")
     rows, cols = state.shape
     vmem = pl.BlockSpec(memory_space=pltpu.VMEM)
     sems = [pltpu.SemaphoreType.DMA((count,))] * 4
+    out_shape = [jax.ShapeDtypeStruct((rows, cols), BF16)]
+    if backward:
+        mixed, weight = product
+        out_shape += [jax.ShapeDtypeStruct((mixed.shape[0], weight.shape[1]), BF16)]
     return pl.pallas_call(
         functools.partial(carry_kernel, count, backward),
-        in_specs=[vmem],
-        out_specs=vmem,
-        out_shape=jax.ShapeDtypeStruct((rows, cols), BF16),
+        in_specs=[vmem] * (1 + len(product)),
+        out_specs=[vmem] * len(out_shape),
+        out_shape=out_shape,
         scratch_shapes=[
             pltpu.VMEM((count, rows // count, cols), BF16),
             pltpu.VMEM((count, rows // count, cols), BF16),
@@ -135,7 +158,7 @@
         + sems,
         compiler_params=params(collective_id=int(backward), has_side_effects=True),
         name="carry_later" if backward else "carry_earlier",
-    )(state)
+    )(state, *product)
 
 
 def forward_kernel(
@@ -203,11 +226,11 @@
 
 
 def project_kernel(
-    go_ref, mixed_ref, normed_ref, radius_ref, fq_ref, weight_ref, gain_ref,
-    result_ref, ga_ref, state_ref, total,
+    go_ref, normed_ref, radius_ref, fq_ref, weight_ref, gain_ref,
+    ga_ref, state_ref, total,
 ):
     step = pl.program_id(0)
-    features = mixed_ref.shape[1]
+    features = normed_ref.shape[1]
     grad_mixed = dot(go_ref[...], weight_ref[...], (1, 1))
     grad_hat = grad_mixed * gain_ref[...]
     normed = normed_ref[...].astype(F32)
@@ -223,15 +246,14 @@
     for head in range(features // HEAD_DIM):
         cols = head_cols(head)
         total[cols, :] += dot(fq_ref[:, cols], grad_att[:, cols], (0, 0))
-    result_ref[...] = dot(mixed_ref[...], weight_ref[...], (1, 0)).astype(BF16)
 
     @pl.when(step == pl.num_programs(0) - 1)
     def _():
         state_ref[...] = total[...].astype(BF16)
 
 
-def project(grad_output, mixed, normed, radius, fq, weight, gain):
-    tokens, features = mixed.shape
+def project(grad_output, normed, radius, fq, weight, gain):
+    tokens, features = normed.shape
     out_cols = weight.shape[1]
     rows = 256
     narrow = pl.BlockSpec((rows, features), lambda i: (i, 0))
@@ -243,22 +265,20 @@
         in_specs=[
             outs,
             narrow,
-            narrow,
             pl.BlockSpec((rows, HEAD_DIM), lambda i: (i, 0)),
             narrow,
             pl.BlockSpec(weight.shape, whole),
             pl.BlockSpec((1, features), whole),
         ],
-        out_specs=[outs, narrow, pl.BlockSpec((features, HEAD_DIM), whole)],
+        out_specs=[narrow, pl.BlockSpec((features, HEAD_DIM), whole)],
         out_shape=[
-            jax.ShapeDtypeStruct((tokens, out_cols), BF16),
             jax.ShapeDtypeStruct((tokens, features), BF16),
             jax.ShapeDtypeStruct((features, HEAD_DIM), BF16),
         ],
         scratch_shapes=[pltpu.VMEM((features, HEAD_DIM), F32)],
         compiler_params=params(),
         name="project",
-    )(grad_output, mixed, normed, radius, fq, weight, gain)
+    )(grad_output, normed, radius, fq, weight, gain)
 
 
 def backward_kernel(
@@ -433,15 +453,23 @@
     part = out_weight.shape[0]
     half_weight = lax.all_gather(out_weight, ("seq", "outer"), axis=0, tiled=True)
     fk, state = local_state(key, value)
-    earlier = carried(state, False)
+    (earlier,) = carried(state, False)
     fq, mixed, normed, radius = forward(query, fk, value, earlier, gain)
     term = pair_term(mixed, grad_result, part)
-    grad_weight = lax.psum_scatter(term, ("seq", "outer"), scatter_dimension=0, tiled=True)
+    outer = lax.axis_index("outer")
+    term = term.reshape(lax.axis_size("seq"), 2, part, term.shape[1])
+    away = lax.dynamic_index_in_dim(term, 1 - outer, 1, False)
+    came = lax.ppermute(away, "outer", [(0, 1), (1, 0)])
+    keep = lax.dynamic_index_in_dim(term, outer, 1, False)
     full_weight = pair_gather(half_weight, part)
-    result, grad_att, grad_state = project(
-        grad_result, mixed, normed, radius, fq, full_weight, gain
-    )
-    later = carried(grad_state, True)
+    grad_att, grad_state = project(
+        grad_result, normed, radius, fq, full_weight, gain
+    )
+    came, grad_state = lax.optimization_barrier((came, grad_state))
+    term = (keep.astype(F32) + came.astype(F32)).astype(BF16).reshape(-1, term.shape[-1])
+    term, grad_state = lax.optimization_barrier((term, grad_state))
+    grad_weight = lax.psum_scatter(term, "seq", scatter_dimension=0, tiled=True)
+    later, result = carried(grad_state, True, mixed, full_weight)
     grad_query, grad_key, grad_value = backward(query, key, value, grad_att, earlier, later)
     return (
         result[None], grad_query[None], grad_key[None], grad_value[None],

time: 208 us -> 231 us (1.11)
  the two profiles are of different devices: /device:TPU:10 before, /device:TPU:0 now
where the time goes in v3:
time: 231 us
  Pallas kernels  145 us (63%)
  waiting for transfers between devices  51.6 us (22%)
  between operations  14.2 us (6%)
  local copies, waits for them, and re-layouts  12.5 us (5%)
  other arithmetic  5.66 us (2%)
    pallas_call x2, Pallas kernels, carried(): pl.pallas_call(functools.partial(carry_kernel, count, backward), in_specs...  81.7 us
    all_gather x1, waiting for transfers between devices, shards(): lax.all_gather(out_weight, ('seq', 'outer'), axis=0, tiled=True)  23.9 us
    reduce_scatter x1, waiting for transfers between devices, shards(): grad_weight = lax.psum_scatter(term, 'seq', scatter_dimension=0, tiled=True)  21.1 us
    pallas_call x1, Pallas kernels, backward(): pl.pallas_call(functools.partial(backward_kernel, group), grid=(features...  16.7 us
    pallas_call x1, Pallas kernels, forward(): pl.pallas_call(functools.partial(forward_kernel, group), grid=(features /...  11.5 us
    pallas_call x1, Pallas kernels, project(): pl.pallas_call(project_kernel, grid=(tokens // rows,), in_specs=[outs, na...  10.9 us
    pallas_call x1, Pallas kernels, pair_gather(): pl.pallas_call(pair_gather_kernel, in_specs=[vmem], out_specs=vmem, out_s...  10.7 us
    pallas_call x1, Pallas kernels, pair_term(): pl.pallas_call(functools.partial(pair_term_kernel, part), in_specs=[vmem,...  10.2 us
  transfers between devices with their start and end apart: 3, of which 3 were waited for; matrix products, arithmetic and copies ran while one was open for 1% of the time, Pallas kernels for 63%

profile of v3, /device:TPU:0, one launch (start us, length us, event | category | flops | bytes accessed | tf_op | source)
XLA Modules:
  0.0 231.0 jit_solution(17471396270410764884)
XLA Ops:
  7.2 0.0 all-gather.2.cloned.1.call-start
  7.2 0.7 all-gather.2.cloned.1.call-update
  7.9 0.0 reduce-scatter.2.cloned.1.call-start
  8.0 0.0 copy-start.1
  8.0 1.6 copy-done.1
  9.5 0.0 copy-start.12
  9.5 3.6 %local_state.1 = (bf16[512,2048]{1,0:T(8,128)(2,1)S(1)}, bf16[2048,128]{1,0:T(8,128)(2,1)S(1)}) custom-call(bf16[512,2048]{1,0:T(8,128)(2,1)S(1)} %bitcast.20, bf16[512,2048]{1,0:T(8,128)(2,1)} %bitcast.30), custom_call_target="tpu_custom_call" | custom-call | tf_op jit(solution)/shard_map/local_state/pallas_call | solution.py:52
  13.2 0.0 copy-start.11
  13.2 1.3 copy-done.11
  14.5 35.6 %carry_earlier.1.state_ref = bf16[2048,128]{1,0:T(8,128)(2,1)S(1)} custom-call(bf16[2048,128]{1,0:T(8,128)(2,1)S(1)} %get-tuple-element.23.refs_0_), custom_call_target="tpu_custom_call" | custom-call | tf_op jit(solution)/shard_map/carry_earlier/pallas_call | solution.py:148
  50.1 0.0 copy-done.12
  50.1 0.0 copy-start
  50.1 11.5 %forward.1 = (bf16[512,2048]{1,0:T(8,128)(2,1)S(1)}, bf16[512,2048]{1,0:T(8,128)(2,1)S(1)}, bf16[512,2048]{1,0:T(8,128)(2,1)}, f32[512,128]{1,0:T(8,128)S(1)}) custom-call(bf16[512,2048]{1,0:T(8,128)(2,1)} %bitcast.22, bf16[512,2048]{1,0:T(8,128)(2,1)} %copy-done.11, bf16[512,2048]{1,0:T(8,128)(2,1)} %bitcast.31, ...), custom_call_target="tpu_custom_call" | custom-call | tf_op jit(solution)/shard_map/forward/pallas_call | solution.py:210
  61.6 0.0 copy-start.4
  61.6 0.0 copy-start.7
  61.6 0.0 copy-done
  61.6 10.2 %pair_term.1 = bf16[8,128,2048]{2,1,0:T(8,128)(2,1)} custom-call(bf16[512,2048]{1,0:T(8,128)(2,1)S(1)} %get-tuple-element.24.mixed_ref.refs_1_, bf16[512,2048]{1,0:T(8,128)(2,1)S(1)} %bitcast.18), custom_call_target="tpu_custom_call" | custom-call | tf_op jit(solution)/shard_map/pair_term/pallas_call | solution.py:430
  71.9 0.0 copy-done.4
  71.9 0.0 copy-done.7
  71.9 3.2 %dynamic-slice_bitcast_fusion = bf16[8,64,2048]{2,1,0:T(8,128)(2,1)} fusion(bf16[8,2,64,2048]{3,2,1,0:T(8,128)(2,1)} %bitcast.33, s32[]{:T(128)S(6)} %select_n.8), kind=kLoop, calls=%fused_computation.2 | loop fusion | bytes 4194308 | tf_op jit(solution)/shard_map/jit(dynamic_index_in_dim)/squeeze | solution.py:461
  75.1 1.5 collective-permute-start
  76.6 23.9 %all-gather.2.cloned.1.call-done = bf16[1024,2048]{1,0:T(8,128)(2,1)} async-done(((bf16[64,2048]{1,0:T(8,128)(2,1)}), bf16[1024,2048]{1,0:T(8,128)(2,1)}) %all-gather.2.cloned.1.call-update) | async-done | bytes 4194320 | tf_op jit(solution)/shard_map/all_gather | solution.py:454
  100.5 0.0 copy-start.6
  100.5 2.2 copy-done.6
  102.7 10.7 %pair_gather.1 = bf16[16,2,64,2048]{3,2,1,0:T(8,128)(2,1)} custom-call(bf16[16,64,2048]{2,1,0:T(8,128)(2,1)S(1)} %bitcast.24), custom_call_target="tpu_custom_call" | custom-call | tf_op jit(solution)/shard_map/pair_gather/pallas_call | solution.py:367
  113.4 0.0 copy-start.13
  113.5 10.9 %project.1 = (bf16[512,2048]{1,0:T(8,128)(2,1)S(1)}, bf16[2048,128]{1,0:T(8,128)(2,1)S(1)}) custom-call(bf16[512,2048]{1,0:T(8,128)(2,1)S(1)} %bitcast.19, bf16[512,2048]{1,0:T(8,128)(2,1)} %get-tuple-element.25.normed_ref, f32[512,128]{1,0:T(8,128)S(1)} %get-tuple-element.26.radius_ref, bf16[512,2048]{1,0:T(8,128)(2,1)} %copy-done.7, ...), custom_call_target="tpu_custom_call" | custom-call | tf_op jit(solution)/shard_map/project/pallas_call | solution.py:262
  124.4 0.0 copy-start.10
  124.4 5.9 %collective-permute-done = bf16[8,64,2048]{2,1,0:T(8,128)(2,1)} collective-permute-done((bf16[8,64,2048]{2,1,0:T(8,128)(2,1)}, bf16[8,64,2048]{2,1,0:T(8,128)(2,1)}, u32[]{:S(2)}, u32[]{:S(2)}) %collective-permute-start) | collective-permute-done | bytes 2097184 | tf_op jit(solution)/shard_map/ppermute | solution.py:462
  130.3 0.0 copy-done.13
  130.3 3.9 %fusion = bf16[8,64,2048]{2,1,0:T(8,128)(2,1)} fusion(bf16[8,64,2048]{2,1,0:T(8,128)(2,1)} %collective-permute-done, bf16[8,2,64,2048]{3,2,1,0:T(8,128)(2,1)S(1)} %bitcast.34, s32[]{:T(128)S(6)} %select_n.7), kind=kLoop, calls=%fused_computation.1 | loop fusion | flops 4194304 | bytes 6291460 | tf_op jit(solution)/shard_map/convert_element_type | solution.py:469
  134.2 0.0 copy-done.10
  134.2 0.0 copy-start.5
  134.2 0.0 reduce-scatter.2.cloned.1.call-update
  134.2 1.6 copy-done.5
  135.8 0.0 copy-start.2
  135.8 0.0 copy-start.3
  135.8 46.1 %carry_later.1 = (bf16[2048,128]{1,0:T(8,128)(2,1)S(1)}, bf16[512,2048]{1,0:T(8,128)(2,1)S(1)}) custom-call(bf16[2048,128]{1,0:T(8,128)(2,1)S(1)} %get-tuple-element.31.refs_0_, bf16[512,2048]{1,0:T(8,128)(2,1)S(1)} %copy-done.5, bf16[2048,2048]{1,0:T(8,128)(2,1)} %bitcast.29), custom_call_target="tpu_custom_call" | custom-call | tf_op jit(solution)/shard_map/carry_later/pallas_call | solution.py:148
  181.8 0.0 copy-start.8
  181.9 1.3 copy-done.8
  183.2 0.0 copy-done.2
  183.2 0.0 copy-done.3
  183.2 0.0 copy-start.9
  183.2 16.7 %backward.1 = (bf16[512,2048]{1,0:T(8,128)(2,1)}, bf16[512,2048]{1,0:T(8,128)(2,1)}, bf16[512,2048]{1,0:T(8,128)(2,1)}) custom-call(bf16[512,2048]{1,0:T(8,128)(2,1)S(1)} %bitcast.23, bf16[512,2048]{1,0:T(8,128)(2,1)S(1)} %bitcast.21, bf16[512,2048]{1,0:T(8,128)(2,1)} %bitcast.32, bf16[512,2048]{1,0:T(8,128)(2,1)} %copy-done.10, ...), custom_call_target="tpu_custom_call" | custom-call | tf_op jit(solution)/shard_map/backward/pallas_call | solution.py:317
  199.9 21.1 %reduce-scatter.2.cloned.1.call-done = bf16[64,2048]{1,0:T(8,128)(2,1)} async-done(((bf16[512,2048]{1,0:T(8,128)(2,1)}), bf16[64,2048]{1,0:T(8,128)(2,1)}) %reduce-scatter.2.cloned.1.call-update) | async-done | bytes 262160 | tf_op jit(solution)/shard_map/reduce_scatter | solution.py:471
  221.0 1.8 convert_element_type.19
  222.8 0.0 copy-done.9
  222.8 1.3 copy.12
Async XLA Ops:
  7.2 93.3 %all-gather.2.cloned.1.call-start = ((), (), s32[]{:S(2)}) async-start(), calls=%async_computation.1 | async-start | bytes 4456448 | tf_op jit(solution)/shard_map/all_gather | solution.py:454
  7.9 213.1 %reduce-scatter.2.cloned.1.call-start = ((), (), s32[]{:S(2)}) async-start(), calls=%async_computation.2 | async-start | bytes 2359296 | tf_op jit(solution)/shard_map/reduce_scatter | solution.py:471
  8.0 1.6 copy-start.1
  9.5 40.6 %copy-start.12 = (f32[2048]{0:T(1024)S(1)}, f32[2048]{0:T(1024)}, u32[]{:S(2)}) copy-start(f32[2048]{0:T(1024)} %param.11) | copy-start | bytes 24580
  13.2 1.3 copy-start.11
  50.1 11.5 %copy-start = (bf16[1,512,2048]{2,1,0:T(8,128)(2,1)S(1)}, bf16[1,512,2048]{2,1,0:T(8,128)(2,1)}, u32[]{:S(2)}) copy-start(bf16[1,512,2048]{2,1,0:T(8,128)(2,1)} %param.9) | copy-start | bytes 6291460
  61.6 10.3 %copy-start.4 = (bf16[512,2048]{1,0:T(8,128)(2,1)}, bf16[512,2048]{1,0:T(8,128)(2,1)S(1)}, u32[]{:S(2)}) copy-start(bf16[512,2048]{1,0:T(8,128)(2,1)S(1)} %get-tuple-element.24.mixed_ref.refs_1_) | copy-start | bytes 6291460
  61.6 10.3 %copy-start.7 = (bf16[512,2048]{1,0:T(8,128)(2,1)}, bf16[512,2048]{1,0:T(8,128)(2,1)S(1)}, u32[]{:S(2)}) copy-start(bf16[512,2048]{1,0:T(8,128)(2,1)S(1)} %get-tuple-element.27.fq_ref) | copy-start | bytes 6291460
  75.1 55.2 %collective-permute-start = (bf16[8,64,2048]{2,1,0:T(8,128)(2,1)}, bf16[8,64,2048]{2,1,0:T(8,128)(2,1)}, u32[]{:S(2)}, u32[]{:S(2)}) collective-permute-start(bf16[8,64,2048]{2,1,0:T(8,128)(2,1)} %dynamic-slice_bitcast_fusion), channel_id=1, source_target_pairs={{0,2},{2,0},{1,3},{3,1},{4,6},{6,4},{5,7},{7,5},{8,10},{10,8},{9,1... | collective-permute-start | bytes 6291464 | tf_op jit(solution)/shard_map/ppermute | solution.py:462
  100.5 2.2 copy-start.6
  113.4 16.8 %copy-start.13 = (bf16[8,128,2048]{2,1,0:T(8,128)(2,1)S(1)}, bf16[8,128,2048]{2,1,0:T(8,128)(2,1)}, u32[]{:S(2)}) copy-start(bf16[8,128,2048]{2,1,0:T(8,128)(2,1)} %pair_term.1) | copy-start | bytes 12582916
  124.4 9.8 %copy-start.10 = (bf16[512,2048]{1,0:T(8,128)(2,1)}, bf16[512,2048]{1,0:T(8,128)(2,1)S(1)}, u32[]{:S(2)}) copy-start(bf16[512,2048]{1,0:T(8,128)(2,1)S(1)} %get-tuple-element.33.ga_ref) | copy-start | bytes 6291460
  134.2 1.6 copy-start.5
  135.8 47.4 %copy-start.2 = (bf16[1,512,2048]{2,1,0:T(8,128)(2,1)S(1)}, bf16[1,512,2048]{2,1,0:T(8,128)(2,1)}, u32[]{:S(2)}) copy-start(bf16[1,512,2048]{2,1,0:T(8,128)(2,1)} %param.7) | copy-start | bytes 6291460
  135.8 47.4 %copy-start.3 = (bf16[1,512,2048]{2,1,0:T(8,128)(2,1)S(1)}, bf16[1,512,2048]{2,1,0:T(8,128)(2,1)}, u32[]{:S(2)}) copy-start(bf16[1,512,2048]{2,1,0:T(8,128)(2,1)} %param.6) | copy-start | bytes 6291460
  181.8 1.3 copy-start.8
  183.2 39.6 %copy-start.9 = (bf16[512,2048]{1,0:T(8,128)(2,1)S(1)}, bf16[512,2048]{1,0:T(8,128)(2,1)}, u32[]{:S(2)}) copy-start(bf16[512,2048]{1,0:T(8,128)(2,1)} %copy-done.8) | copy-start | bytes 6291460
Sparse Core Ops, SparseCore 0:
  10.8 89.7 all-gather.1
  134.3 86.6 reduce-scatter.1
